TPU v7x, 128 devices: a whole 4x4x4 slice. The times are simulated.
128 devices in a mesh: src: 16 (over y, x), obs: 8 (over z, core).
Axes of the slice: x: 4, y: 4, z: 4, core: 2. Of those that a mesh axis runs over, the one named last changes fastest.
Arguments:
- history: bfloat16 [8, 128, 256, 128], P(None, 'src'), may hold values from -6 to 6
- tiles: bfloat16 [8192, 256, 256], P(('src', 'obs')), may hold values from -0.0390625 to 0.0390625
- tile_obs: int32 [8192], P(('src', 'obs')), may hold values from 0 to 15
- tile_src: int32 [8192], P(('src', 'obs')), may hold values from 0 to 7
- tile_lag: int32 [8192], P(('src', 'obs')), may hold values from 1 to 8
- help_tiles: bfloat16 [3072, 256, 256], P(('src', 'obs')), may hold values from -0.0390625 to 0.0390625
- help_obs: int32 [3072], P(('src', 'obs')), may hold values from 0 to 15
- help_src: int32 [3072], replicated, may hold values from 0 to 127, as said below
- help_lag: int32 [3072], replicated, may hold values from 4 to 8
- self_inverse: float32 [128, 256, 256], P(('src', 'obs')), may hold values from -0.375 to 0.375
- excitation: bfloat16 [4, 128, 256, 128], P(None, ('src', 'obs')), may hold values from -6 to 6
Outputs:
- currents: bfloat16 [4, 128, 256, 128], P(None, ('src', 'obs'))
Inputs may be any that keep to these rules, and one draw needn't show every extreme that they name: `help_src`: each device's block of 24 entries names source groups outside the device's own source row; at most 4 of them lie in any one source row, and exactly 4 in some row.
All inputs are finite; a program needn't handle non-finite values.
Results may differ from a plain program's by a relative error of at most 0.003.
Values may be sent and summed in bfloat16 or wider, within the bound.
A program may use at most 192 MiB of HBM per device.

v0:
```python
import jax
import jax.numpy as jnp
from jax import lax
from jax.sharding import PartitionSpec as P

LAGS = 8
STEPS = 4
HELP_DEV = 24
CAP = 4


def request_table(help_src, help_lag, n_src, n_obs, column, source_count):
    all_src = help_src.reshape(n_src, n_obs, HELP_DEV)
    all_lag = help_lag.reshape(n_src, n_obs, HELP_DEV)
    req_src = lax.dynamic_index_in_dim(all_src, column, 1, keepdims=False)
    req_lag = lax.dynamic_index_in_dim(all_lag, column, 1, keepdims=False)
    req_row = req_src // source_count
    order = jnp.arange(HELP_DEV, dtype=jnp.int32)
    earlier = (req_row[:, :, None] == req_row[:, None, :]) & (
        order[None, None, :] < order[None, :, None]
    )
    req_slot = jnp.sum(earlier.astype(jnp.int32), axis=2)
    return (req_src, req_lag, req_row, req_slot)


def build_send(flat_history, req_src, req_lag, req_row, req_slot, row_here, step, source_count):
    slots = jnp.arange(CAP, dtype=jnp.int32)
    match = (req_row[:, None, :] == row_here) & (req_slot[:, None, :] == slots[None, :, None])
    flat_index = (LAGS + step - req_lag) * source_count + req_src % source_count
    index = jnp.sum(jnp.where(match, flat_index[:, None, :], 0), axis=2)
    valid = jnp.any(match, axis=2)
    picked = jnp.take(flat_history, index.reshape(-1), axis=0)
    picked = picked.reshape(index.shape + flat_history.shape[1:])
    return jnp.where(valid[:, :, None, None], picked, jnp.zeros_like(picked))


def on_device(
    history,
    tiles,
    tile_obs,
    tile_src,
    tile_lag,
    help_tiles,
    help_obs,
    help_src,
    help_lag,
    self_inverse,
    excitation,
):
    n_src = lax.axis_size("src")
    n_obs = lax.axis_size("obs")
    row_here = lax.axis_index("src")
    column = lax.axis_index("obs")
    source_count = history.shape[1]
    group_size = history.shape[2]
    columns_rhs = history.shape[3]
    own_groups = self_inverse.shape[0]
    slab_count = own_groups * n_src
    flat_history = history.reshape(LAGS * source_count, group_size, columns_rhs)
    req_src, req_lag, req_row, req_slot = request_table(
        help_src, help_lag, n_src, n_obs, column, source_count
    )
    mine_row = lax.dynamic_index_in_dim(req_row, row_here, 0, keepdims=False)
    mine_slot = lax.dynamic_index_in_dim(req_slot, row_here, 0, keepdims=False)
    pick_index = mine_row * CAP + mine_slot
    slab_ids = jnp.arange(slab_count, dtype=jnp.int32)
    onehot_own = (tile_obs[None, :] == slab_ids[:, None]).astype(jnp.float32)
    onehot_aid = (help_obs[None, :] == slab_ids[:, None]).astype(jnp.float32)
    table = jnp.concatenate(
        [history, jnp.zeros((STEPS,) + history.shape[1:], history.dtype)], axis=0
    )
    solved_steps = []
    for step in range(STEPS):
        send = build_send(
            flat_history, req_src, req_lag, req_row, req_slot, row_here, step, source_count
        )
        received = lax.all_to_all(send, "src", split_axis=0, concat_axis=0, tiled=True)
        aid_slices = jnp.take(
            received.reshape(n_src * CAP, group_size, columns_rhs), pick_index, axis=0
        )
        flat_table = table.reshape((LAGS + STEPS) * source_count, group_size, columns_rhs)
        own_index = (LAGS + step - tile_lag) * source_count + tile_src
        own_slices = jnp.take(flat_table, own_index, axis=0)
        prod_own = jnp.einsum("tab,tbr->tar", tiles, own_slices, preferred_element_type=jnp.float32)
        prod_aid = jnp.einsum(
            "tab,tbr->tar", help_tiles, aid_slices, preferred_element_type=jnp.float32
        )
        slab = jnp.dot(
            onehot_own, prod_own.reshape(prod_own.shape[0], -1), precision=lax.Precision.HIGHEST
        )
        slab = slab + jnp.dot(
            onehot_aid, prod_aid.reshape(prod_aid.shape[0], -1), precision=lax.Precision.HIGHEST
        )
        field = lax.psum_scatter(
            slab.reshape(slab_count, group_size, columns_rhs),
            "src",
            scatter_dimension=0,
            tiled=True,
        )
        rhs = excitation[step].astype(jnp.float32) - field
        solved = jnp.einsum(
            "gab,gbr->gar", self_inverse, rhs, precision=lax.Precision.HIGHEST
        ).astype(jnp.bfloat16)
        solved_steps.append(solved)
        if step + 1 < STEPS:
            row_slices = lax.all_gather(solved, "obs", axis=0, tiled=True)
            table = lax.dynamic_update_index_in_dim(table, row_slices, LAGS + step, 0)
    return jnp.stack(solved_steps, axis=0)


def solution(mesh):
    placed = (
        P(None, "src", None, None),
        P(("src", "obs"), None, None),
        P(("src", "obs")),
        P(("src", "obs")),
        P(("src", "obs")),
        P(("src", "obs"), None, None),
        P(("src", "obs")),
        P(),
        P(),
        P(("src", "obs"), None, None),
        P(None, ("src", "obs"), None, None),
    )
    return jax.shard_map(
        on_device,
        mesh=mesh,
        in_specs=placed,
        out_specs=P(None, ("src", "obs"), None, None),
        check_vma=False,
    )
```

profile of v0, /device:TPU:1, one launch (start us, length us, event | category | flops | bytes accessed | tf_op | source)
XLA Modules:
  0.0 742.3 jit_solution(795271405779394223)
XLA Ops:
  15.6 5.3 gather_fusion.4
  20.9 5.3 gather_fusion.7
  26.3 5.3 gather_fusion.10
  42.3 7.5 %broadcast_select_fusion.4 = (bf16[16,4,256,128]{3,2,1,0:T(8,128)(2,1)}, bf16[16,4,256,128]{3,2,1,0:T(8,128)(2,1)}, bf16[16,4,256,128]{3,2,1,0:T(8,128)(2,1)}, bf16[16,4,256,128]{3,2,1,0:T(8,128)(2,1)}) fusion(bf16[16,4,256,128]{3,2,1,0:T(8,128)(2,1)} %bitcast.178, pred[16,4]{1,0:T(8,128)(4,1)S(1)} %copy.78, bf16[16,4,256,128]{3,2,1,0:T(8,128)(2,1)S(1)} %bitcast.176, ...), kind=kLoop, calls=%fused_computation.44 | loop fusion | flops 8388608 | bytes 33554496 | tf_op jit(solution)/shard_map/jit(_where)/select_n | solution.py:34
  49.9 7.8 %all-to-all-start = ((bf16[16,4,256,128]{3,2,1,0:T(8,128)(2,1)}), bf16[16,4,256,128]{3,2,1,0:T(8,128)(2,1)}, u32[]{:S(2)}, u32[]{:S(2)}) async-start(bf16[16,4,256,128]{3,2,1,0:T(8,128)(2,1)} %get-tuple-element.34), calls=%async_computation | async-start | bytes 8388608 | tf_op jit(solution)/shard_map/all_to_all | solution.py:77
  57.7 6.0 concatenate.3
  63.7 5.8 gather_fusion
  69.6 12.6 %fusion.24 = f32[64,256,128]{1,2,0:T(8,128)} fusion(bf16[64,256,256]{2,1,0:T(8,128)(2,1)} %param.18, bf16[64,256,128]{2,1,0:T(8,128)(2,1)} %gather_fusion, pred[64]{0:T(512)(128)(4,1)S(1)} %get-tuple-element.37), kind=kOutput, calls=%fused_computation.48 | convolution fusion | flops 1075838976 | bytes 20971584 | tf_op jit(solution)/shard_map/tab,tbr->tar/dot_general | solution.py:84
  82.2 9.0 %copy.77 = f32[64,256,128]{2,1,0:T(8,128)} copy(f32[64,256,128]{1,2,0:T(8,128)} %fusion.24) | data formatting | bytes 16777216 | tf_op jit(solution)/shard_map/tab,tbr->tar/dot_general | solution.py:84
  91.2 11.8 %fusion.9 = f32[16,32768]{1,0:T(8,128)} fusion(f32[8,8,256,128]{3,2,1,0:T(8,128)} %bitcast.171, s32[64]{0:T(128)S(1)} %copy-done.9), kind=kOutput, calls=%fused_computation.25 | convolution fusion | flops 402654208 | bytes 10486016 | tf_op jit(solution)/shard_map/dot_general | solution.py:88
  103.0 17.1 %all-to-all-done = bf16[16,4,256,128]{3,2,1,0:T(8,128)(2,1)} async-done(((bf16[16,4,256,128]{3,2,1,0:T(8,128)(2,1)}), bf16[16,4,256,128]{3,2,1,0:T(8,128)(2,1)}, u32[]{:S(2)}, u32[]{:S(2)}) %all-to-all-start) | async-done | bytes 4194336 | tf_op jit(solution)/shard_map/all_to_all | solution.py:77
  137.7 5.6 fusion.48
  145.1 40.5 %all-to-all-done.1 = bf16[16,4,256,128]{3,2,1,0:T(8,128)(2,1)} async-done(((bf16[16,4,256,128]{3,2,1,0:T(8,128)(2,1)}), bf16[16,4,256,128]{3,2,1,0:T(8,128)(2,1)}, u32[]{:S(2)}, u32[]{:S(2)}) %all-to-all-start.1) | async-done | bytes 4194336 | tf_op jit(solution)/shard_map/all_to_all | solution.py:77
  203.0 76.3 %reduce-scatter.13.cloned.1.call-done = f32[1,256,128]{2,1,0:T(8,128)} async-done(((f32[16,256,128]{2,1,0:T(8,128)}), f32[1,256,128]{2,1,0:T(8,128)}) %reduce-scatter.13.cloned.1.call-update) | async-done | bytes 131088
  280.6 16.8 %all-gather = bf16[2048,128]{0,1:T(8,128)(2,1)} all-gather(bf16[256,128]{0,1:T(8,128)(2,1)S(1)} %bitcast.190), channel_id=2, replica_groups=mesh['src'=16,'obs'=8] {'obs'}, dimensions={0}, use_global_device_ids=true | all-gather | bytes 589824 | tf_op jit(solution)/shard_map/all_gather | solution.py:106
  301.4 5.8 gather_fusion.3
  307.2 12.7 %fusion.27 = f32[64,256,128]{1,2,0:T(8,128)} fusion(bf16[64,256,256]{2,1,0:T(8,128)(2,1)} %param.18, bf16[64,256,128]{2,1,0:T(8,128)(2,1)} %gather_fusion.3, pred[64]{0:T(512)(128)(4,1)S(1)} %get-tuple-element.35), kind=kOutput, calls=%fused_computation.49 | convolution fusion | flops 1075838976 | bytes 20971584 | tf_op jit(solution)/shard_map/tab,tbr->tar/dot_general | solution.py:84
  319.9 9.5 %copy.84 = f32[64,256,128]{2,1,0:T(8,128)} copy(f32[64,256,128]{1,2,0:T(8,128)} %fusion.27) | data formatting | bytes 16777216 | tf_op jit(solution)/shard_map/tab,tbr->tar/dot_general | solution.py:84
  329.4 10.8 %fusion.6 = f32[16,32768]{1,0:T(8,128)S(1)} fusion(f32[8,8,256,128]{3,2,1,0:T(8,128)} %bitcast.172, s32[64]{0:T(128)S(1)} %copy-done.9), kind=kOutput, calls=%fused_computation.22 | convolution fusion | flops 402654208 | bytes 10486016 | tf_op jit(solution)/shard_map/dot_general | solution.py:88
  363.1 95.3 %reduce-scatter.15.cloned.1.call-done = f32[1,256,128]{2,1,0:T(8,128)} async-done(((f32[16,256,128]{2,1,0:T(8,128)}), f32[1,256,128]{2,1,0:T(8,128)}) %reduce-scatter.15.cloned.1.call-update) | async-done | bytes 131088
  459.8 17.0 %all-gather.1 = bf16[2048,128]{0,1:T(8,128)(2,1)} all-gather(bf16[256,128]{0,1:T(8,128)(2,1)S(1)} %bitcast.192), channel_id=3, replica_groups=mesh['src'=16,'obs'=8] {'obs'}, dimensions={0}, use_global_device_ids=true | all-gather | bytes 589824 | tf_op jit(solution)/shard_map/all_gather | solution.py:106
  480.8 6.1 gather_fusion.6
  486.9 12.7 %fusion.30 = f32[64,256,128]{1,2,0:T(8,128)} fusion(bf16[64,256,256]{2,1,0:T(8,128)(2,1)} %param.18, bf16[64,256,128]{2,1,0:T(8,128)(2,1)} %gather_fusion.6, pred[64]{0:T(512)(128)(4,1)} %get-tuple-element.39), kind=kOutput, calls=%fused_computation.50 | convolution fusion | flops 1075838976 | bytes 20971584 | tf_op jit(solution)/shard_map/tab,tbr->tar/dot_general | solution.py:84
  499.5 9.0 %copy.90 = f32[64,256,128]{2,1,0:T(8,128)} copy(f32[64,256,128]{1,2,0:T(8,128)} %fusion.30) | data formatting | bytes 16777216 | tf_op jit(solution)/shard_map/tab,tbr->tar/dot_general | solution.py:84
  508.5 10.8 %fusion.3 = f32[16,32768]{1,0:T(8,128)S(1)} fusion(f32[8,8,256,128]{3,2,1,0:T(8,128)} %bitcast.173, s32[64]{0:T(128)S(1)} %copy-done.9), kind=kOutput, calls=%fused_computation.19 | convolution fusion | flops 402654208 | bytes 10486016 | tf_op jit(solution)/shard_map/dot_general | solution.py:88
  538.2 56.9 %reduce-scatter.17.cloned.1.call-done = f32[1,256,128]{2,1,0:T(8,128)} async-done(((f32[16,256,128]{2,1,0:T(8,128)}), f32[1,256,128]{2,1,0:T(8,128)}) %reduce-scatter.17.cloned.1.call-update) | async-done | bytes 131088
  597.0 17.1 %all-gather.2 = bf16[2048,128]{0,1:T(8,128)(2,1)} all-gather(bf16[256,128]{0,1:T(8,128)(2,1)S(1)} %bitcast.194), channel_id=4, replica_groups=mesh['src'=16,'obs'=8] {'obs'}, dimensions={0}, use_global_device_ids=true | all-gather | bytes 589824 | tf_op jit(solution)/shard_map/all_gather | solution.py:106
  618.1 6.1 gather_fusion.9
  624.2 12.6 %fusion.33 = f32[64,256,128]{1,2,0:T(8,128)} fusion(bf16[64,256,256]{2,1,0:T(8,128)(2,1)} %param.18, bf16[64,256,128]{2,1,0:T(8,128)(2,1)} %gather_fusion.9, pred[64]{0:T(512)(128)(4,1)S(1)} %copy-done.11), kind=kOutput, calls=%fused_computation.51 | convolution fusion | flops 1075838976 | bytes 20971584 | tf_op jit(solution)/shard_map/tab,tbr->tar/dot_general | solution.py:84
  636.8 9.1 %copy.96 = f32[64,256,128]{2,1,0:T(8,128)} copy(f32[64,256,128]{1,2,0:T(8,128)} %fusion.33) | data formatting | bytes 16777216 | tf_op jit(solution)/shard_map/tab,tbr->tar/dot_general | solution.py:84
  645.9 10.8 %fusion = f32[16,32768]{1,0:T(8,128)S(1)} fusion(f32[8,8,256,128]{3,2,1,0:T(8,128)} %bitcast.174, s32[64]{0:T(128)S(1)} %copy-done.9), kind=kOutput, calls=%fused_computation.16 | convolution fusion | flops 402654208 | bytes 10486016 | tf_op jit(solution)/shard_map/dot_general | solution.py:88
  661.7 70.9 %reduce-scatter.19.cloned.1.call-done = f32[1,256,128]{2,1,0:T(8,128)} async-done(((f32[16,256,128]{2,1,0:T(8,128)}), f32[1,256,128]{2,1,0:T(8,128)}) %reduce-scatter.19.cloned.1.call-update) | async-done | bytes 131088
  (112 shorter events, 122.7 us)
Async XLA Ops:
  6.5 122.6 %copy-start = (bf16[24,256,256]{2,1,0:T(8,128)(2,1)S(1)}, bf16[24,256,256]{2,1,0:T(8,128)(2,1)}, u32[]{:S(2)}) copy-start(bf16[24,256,256]{2,1,0:T(8,128)(2,1)} %param.22) | copy-start | bytes 9437188
  26.3 5.3 copy-start.12
  26.3 5.3 copy-start.13
  32.1 3.4 copy-start.3
  35.5 2.2 copy-start.1
  37.7 2.2 copy-start.2
  49.9 70.3 %all-to-all-start = ((bf16[16,4,256,128]{3,2,1,0:T(8,128)(2,1)}), bf16[16,4,256,128]{3,2,1,0:T(8,128)(2,1)}, u32[]{:S(2)}, u32[]{:S(2)}) async-start(bf16[16,4,256,128]{3,2,1,0:T(8,128)(2,1)} %get-tuple-element.34), calls=%async_computation | async-start | bytes 8388608 | tf_op jit(solution)/shard_map/all_to_all | solution.py:77
  82.2 9.1 %copy-start.9 = (s32[64]{0:T(128)S(1)}, s32[64]{0:T(128)}, u32[]{:S(2)}) copy-start(s32[64]{0:T(128)} %param.19) | copy-start | bytes 772
  120.2 65.4 %all-to-all-start.1 = ((bf16[16,4,256,128]{3,2,1,0:T(8,128)(2,1)}), bf16[16,4,256,128]{3,2,1,0:T(8,128)(2,1)}, u32[]{:S(2)}, u32[]{:S(2)}) async-start(bf16[16,4,256,128]{3,2,1,0:T(8,128)(2,1)} %get-tuple-element.32), calls=%async_computation.1 | async-start | bytes 8388608 | tf_op jit(solution)/shard_map/all_to_all | solution.py:77
  124.7 154.6 %reduce-scatter.13.cloned.1.call-start = ((), (), s32[]{:S(2)}) async-start(), calls=%async_computation.8 | async-start | bytes 2228224
  134.1 3.6 copy-start.10
  185.6 160.2 %all-to-all-start.2 = ((bf16[16,4,256,128]{3,2,1,0:T(8,128)(2,1)}), bf16[16,4,256,128]{3,2,1,0:T(8,128)(2,1)}, u32[]{:S(2)}, u32[]{:S(2)}) async-start(bf16[16,4,256,128]{3,2,1,0:T(8,128)(2,1)} %get-tuple-element.33), calls=%async_computation.2 | async-start | bytes 8388608 | tf_op jit(solution)/shard_map/all_to_all | solution.py:77
  190.2 268.3 %reduce-scatter.15.cloned.1.call-start = ((), (), s32[]{:S(2)}) async-start(), calls=%async_computation.9 | async-start | bytes 2228224
  199.4 79.9 %copy-start.7 = (f32[1,256,256]{2,1,0:T(8,128)S(1)}, f32[1,256,256]{2,1,0:T(8,128)}, u32[]{:S(2)}) copy-start(f32[1,256,256]{2,1,0:T(8,128)} %param.26) | copy-start | bytes 786436
  329.4 10.8 %copy-start.5 = (f32[24,256,128]{2,1,0:T(8,128)S(1)}, f32[24,256,128]{2,1,0:T(8,128)}, u32[]{:S(2)}) copy-start(f32[24,256,128]{2,1,0:T(8,128)} %copy.87) | copy-start | bytes 9437188
  345.8 179.8 %all-to-all-start.3 = ((bf16[16,4,256,128]{3,2,1,0:T(8,128)(2,1)}), bf16[16,4,256,128]{3,2,1,0:T(8,128)(2,1)}, u32[]{:S(2)}, u32[]{:S(2)}) async-start(bf16[16,4,256,128]{3,2,1,0:T(8,128)(2,1)} %get-tuple-element.31), calls=%async_computation.3 | async-start | bytes 8388608 | tf_op jit(solution)/shard_map/all_to_all | solution.py:77
  350.4 244.7 %reduce-scatter.17.cloned.1.call-start = ((), (), s32[]{:S(2)}) async-start(), calls=%async_computation.10 | async-start | bytes 2228224
  508.5 10.8 %copy-start.6 = (f32[24,256,128]{2,1,0:T(8,128)S(1)}, f32[24,256,128]{2,1,0:T(8,128)}, u32[]{:S(2)}) copy-start(f32[24,256,128]{2,1,0:T(8,128)} %copy.93) | copy-start | bytes 9437188
  524.2 208.3 %reduce-scatter.19.cloned.1.call-start = ((), (), s32[]{:S(2)}) async-start(), calls=%async_computation.11 | async-start | bytes 2228224
  596.4 0.6 copy-start.8
  618.1 6.1 copy-start.11
  645.9 10.8 %copy-start.4 = (f32[24,256,128]{2,1,0:T(8,128)S(1)}, f32[24,256,128]{2,1,0:T(8,128)}, u32[]{:S(2)}) copy-start(f32[24,256,128]{2,1,0:T(8,128)} %copy.99) | copy-start | bytes 9437188
Sparse Core Ops, SparseCore 0:
  145.2 134.0 reduce-scatter.12
  345.3 113.1 reduce-scatter.14
  524.4 70.6 reduce-scatter.16
  661.8 70.6 reduce-scatter.18
where the time goes:
time: 751 us; the launch traced here: 742 us
  waiting for transfers between devices  357 us (48%)
  local copies, waits for them, and re-layouts  146 us (19%)
  matrix products  135 us (18%)
  blocking collectives  50.9 us (7%)
  starting transfers between devices  22 us (3%)
  other arithmetic  18.1 us (2%)
  between operations  13.7 us (2%)
    unnamed x8, waiting for transfers between devices  299 us
    all_to_all x4, waiting for transfers between devices, on_device(): lax.all_to_all(send, 'src', split_axis=0, concat_axis=0, tiled=True)  57.6 us
    all_gather x3, blocking collectives, on_device(): row_slices = lax.all_gather(solved, 'obs', axis=0, tiled=True)  50.9 us
    dot_general x4, matrix products, on_device(): jnp.einsum('tab,tbr->tar', tiles, own_slices, preferred_element_type=jnp....  50.6 us
    dot_general x4, matrix products, on_device(): jnp.dot(onehot_own, prod_own.reshape(prod_own.shape[0], -1), precision=la...  44.1 us
    dot_general x4, local copies, waits for them, and re-layouts, on_device(): jnp.einsum('tab,tbr->tar', tiles, own_slices, preferred_element_type=jnp....  36.6 us
    gather x4, local copies, waits for them, and re-layouts, on_device(): own_slices = jnp.take(flat_table, own_index, axis=0)  23.8 us
    all_to_all x4, starting transfers between devices, on_device(): lax.all_to_all(send, 'src', split_axis=0, concat_axis=0, tiled=True)  21.6 us
  transfers between devices with their start and end apart: 8, of which 6 were waited for; matrix products, arithmetic and copies ran while one was open for 27% of the time, Pallas kernels for 0%

commit v1 on v0

v1 whole, which is shorter than its diff:
```python
import functools

import jax
import jax.numpy as jnp
from jax import lax
from jax.experimental import pallas as pl
from jax.experimental.pallas import tpu as pltpu
from jax.sharding import PartitionSpec as P

LAGS = 8
STEPS = 4
SIDE = 4
ROWS = 16
COLS = 8
GROUP = 256
RHS = 128
OWN = 64
HELP = 24
CAP = 4
POOL = ROWS * CAP
MESH = pl.DeviceIdType.MESH
F32 = jnp.float32
BF16 = jnp.bfloat16
VMEM_LIMIT = 60 * 2**20


def history_kernel(
    own_obs, own_src, own_lag, aid_ok, aid_obs, aid_src, aid_lag,
    history, tiles, pool, out, past, own_buf, aid_buf, acc, sem_past, sem_own, sem_aid, sem_out,
):
    chunk = 8
    past_copies = [
        pltpu.make_async_copy(
            history.at[p], past.at[:, :, pl.ds(p * RHS, RHS)], sem_past.at[p]
        )
        for p in range(LAGS)
    ]
    own_copies = [
        pltpu.make_async_copy(
            tiles.at[pl.ds(i * chunk, chunk)], own_buf.at[pl.ds(i * chunk, chunk)], sem_own.at[i]
        )
        for i in range(OWN // chunk)
    ]
    aid_copies = [
        pltpu.make_async_copy(
            pool.at[pl.ds(i * chunk, chunk)], aid_buf.at[pl.ds(i * chunk, chunk)], sem_aid.at[i]
        )
        for i in range(POOL // chunk)
    ]
    for copy in past_copies + own_copies + aid_copies:
        copy.start()
    past[:, :, pl.ds(LAGS * RHS, 3 * RHS)] = jnp.zeros((COLS, GROUP, 3 * RHS), BF16)
    acc[...] = jnp.zeros(acc.shape, F32)
    for copy in past_copies:
        copy.wait()

    def add(tile, obs, src, lag):
        first = pl.multiple_of((LAGS - lag) * RHS, RHS)
        window = past[src, :, pl.ds(first, STEPS * RHS)]
        acc[obs] += jnp.dot(tile, window, preferred_element_type=F32)

    for i in range(OWN // chunk):
        own_copies[i].wait()

        @pl.loop(i * chunk, (i + 1) * chunk)
        def _(t):
            add(own_buf[t], own_obs[t], own_src[t], own_lag[t])

    for i in range(POOL // chunk):
        aid_copies[i].wait()

        @pl.loop(i * chunk, (i + 1) * chunk)
        def _(t):
            @pl.when(aid_ok[t] != 0)
            def _():
                add(aid_buf[t], aid_obs[t], aid_src[t], aid_lag[t])

    copy = pltpu.make_async_copy(acc, out, sem_out)
    copy.start()
    copy.wait()


def history_fields(own_meta, aid_meta, history, tiles, pool):
    smem = pl.BlockSpec(memory_space=pltpu.SMEM)
    hbm = pl.BlockSpec(memory_space=pl.ANY)
    return pl.pallas_call(
        history_kernel,
        out_shape=jax.ShapeDtypeStruct((ROWS, GROUP, STEPS * RHS), F32),
        in_specs=[smem] * 7 + [hbm] * 3,
        out_specs=hbm,
        scratch_shapes=[
            pltpu.VMEM((COLS, GROUP, (LAGS + 3) * RHS), BF16),
            pltpu.VMEM((OWN, GROUP, GROUP), BF16),
            pltpu.VMEM((POOL, GROUP, GROUP), BF16),
            pltpu.VMEM((ROWS, GROUP, STEPS * RHS), F32),
            pltpu.SemaphoreType.DMA((LAGS,)),
            pltpu.SemaphoreType.DMA((OWN // 8,)),
            pltpu.SemaphoreType.DMA((POOL // 8,)),
            pltpu.SemaphoreType.DMA,
        ],
        compiler_params=pltpu.CompilerParams(vmem_limit_bytes=VMEM_LIMIT),
    )(*own_meta, *aid_meta, history, tiles, pool)


def march_kernel(
    perm, index, keep, last, slab_hbm, tiles_hbm, inverse, excitation, out,
    slab, tiles, table, cur0, cur1, cur2, seg, mine,
    tx1, rx1, tx2, rx2,
    sem_slab, sem_tiles, s_tx1, s_rx1, s_tx2, s_rx2, s_ztx, s_zrx, s_ctx, s_crx,
):
    row = lax.axis_index("src")
    col = lax.axis_index("obs")
    y, x = row // SIDE, lax.rem(row, SIDE)
    z, core = col // 2, lax.rem(col, 2)
    half = GROUP // 2
    cur = [cur0, cur1, cur2]

    def turn(v, d):
        return lax.rem(v + d + SIDE, SIDE)

    def plane(yy, xx):
        return (yy * SIDE + xx, col)

    partners = (
        [plane(y, turn(x, d)) for d in (1, 2, 3)]
        + [plane(turn(y, d), x) for d in (1, 2, 3)]
        + [(row, turn(z, d) * 2 + core) for d in (1, 2, 3)]
        + [(row, z * 2 + 1 - core)]
    )
    slab_copy = pltpu.make_async_copy(slab_hbm, slab, sem_slab)
    tiles_copy = pltpu.make_async_copy(tiles_hbm, tiles, sem_tiles)
    slab_copy.start()
    tiles_copy.start()
    barrier = pltpu.get_barrier_semaphore()
    for device in partners:
        pl.semaphore_signal(barrier, inc=1, device_id=device, device_id_type=MESH)
    table[3 * COLS] = jnp.zeros((GROUP, RHS), BF16)
    seg[OWN] = jnp.zeros((GROUP, RHS), F32)
    slab_copy.wait()
    pl.semaphore_wait(barrier, len(partners))
    sent = []

    for step in range(STEPS):
        if step:

            def product(k, carry):
                term = jnp.dot(
                    tiles[perm[k]],
                    table[index[(step - 1) * OWN + k]],
                    preferred_element_type=F32,
                )
                total = carry * keep[k] + term
                seg[k] = total
                return total

            lax.fori_loop(0, OWN, product, jnp.zeros((GROUP, RHS), F32))

        def field(obs, part):
            value = slab[obs, pl.ds(part * half, half), pl.ds(step * RHS, RHS)]
            if step:
                value = value + seg[last[obs], pl.ds(part * half, half), :]
            return value

        def owner(part, other, along):
            return other * SIDE + along if part == 0 else along * SIDE + other

        def toward(part, along):
            return plane(y, along) if part == 0 else plane(along, x)

        here = (x, y)
        first = {}
        for d in (2, 1, 3):
            for part in (0, 1):
                along = turn(here[part], d)
                for other in range(SIDE):
                    tx1[step, part, d - 1, other] = field(
                        owner(part, other, along), part
                    ).astype(BF16)
                copy = pltpu.make_async_remote_copy(
                    src_ref=tx1.at[step, part, d - 1],
                    dst_ref=rx1.at[step, part, d - 1],
                    send_sem=s_tx1.at[step, part, d - 1],
                    recv_sem=s_rx1.at[step, part, d - 1],
                    device_id=toward(part, along),
                    device_id_type=MESH,
                )
                copy.start()
                first[part, d] = copy
                sent.append(copy)
        second = {}
        for part in (0, 1):
            for d in (1, 3, 2):
                first[part, d].wait_recv()

            def summed(other):
                value = field(owner(part, other, here[part]), part)
                for d in (1, 2, 3):
                    value = value + rx1[step, part, d - 1, other].astype(F32)
                return value

            for d in (2, 1, 3):
                other = turn(here[1 - part], d)
                tx2[step, part, d - 1] = summed(other)
                copy = pltpu.make_async_remote_copy(
                    src_ref=tx2.at[step, part, d - 1],
                    dst_ref=rx2.at[step, part, d - 1],
                    send_sem=s_tx2.at[step, part, d - 1],
                    recv_sem=s_rx2.at[step, part, d - 1],
                    device_id=toward(1 - part, other),
                    device_id_type=MESH,
                )
                copy.start()
                second[part, d] = copy
                sent.append(copy)
            mine[pl.ds(part * half, half), :] = summed(here[1 - part])
        for part in (0, 1):
            rows = pl.ds(part * half, half)
            value = mine[rows, :]
            for d in (1, 3, 2):
                second[part, d].wait_recv()
                value = value + rx2[step, part, d - 1]
            mine[rows, :] = excitation[step, 0, rows, :].astype(F32) - value
        solved = jnp.dot(
            inverse[0], mine[...], precision=lax.Precision.HIGHEST, preferred_element_type=F32
        ).astype(BF16)
        out[step, 0] = solved
        if step == STEPS - 1:
            break
        now = cur[step]
        now[col] = solved

        def along_z(e):
            return pltpu.make_async_remote_copy(
                src_ref=now.at[col],
                dst_ref=now.at[col],
                send_sem=s_ztx.at[step, e - 1],
                recv_sem=s_zrx.at[step, e - 1],
                device_id=(row, turn(z, e) * 2 + core),
                device_id_type=MESH,
            )

        def to_sibling(e):
            block = turn(z, -e) * 2 + core
            return pltpu.make_async_remote_copy(
                src_ref=now.at[block],
                dst_ref=now.at[block],
                send_sem=s_ctx.at[step, e],
                recv_sem=s_crx.at[step, e],
                device_id=(row, z * 2 + 1 - core),
                device_id_type=MESH,
            )

        spread = {e: along_z(e) for e in (1, 2, 3)}
        across = {e: to_sibling(e) for e in range(SIDE)}
        for e in (2, 1, 3):
            spread[e].start()
        across[0].start()
        for e in (1, 3, 2):
            spread[e].wait_recv()
            across[e].start()
        if step == 0:
            tiles_copy.wait()
        for e in (0, 1, 3, 2):
            across[e].wait_recv()
        table[pl.ds(step * COLS, COLS)] = now[...]
        sent += list(spread.values()) + list(across.values())
    for copy in sent:
        copy.wait_send()


def march(perm, index, keep, last, slab, tiles, inverse, excitation):
    smem = pl.BlockSpec(memory_space=pltpu.SMEM)
    hbm = pl.BlockSpec(memory_space=pl.ANY)
    vmem = pl.BlockSpec(memory_space=pltpu.VMEM)
    half = GROUP // 2
    dma = pltpu.SemaphoreType.DMA
    return pl.pallas_call(
        march_kernel,
        out_shape=jax.ShapeDtypeStruct((STEPS, 1, GROUP, RHS), BF16),
        in_specs=[smem] * 4 + [hbm] * 2 + [vmem] * 2,
        out_specs=vmem,
        scratch_shapes=[
            pltpu.VMEM((ROWS, GROUP, STEPS * RHS), F32),
            pltpu.VMEM((OWN, GROUP, GROUP), BF16),
            pltpu.VMEM((3 * COLS + 1, GROUP, RHS), BF16),
            pltpu.VMEM((COLS, GROUP, RHS), BF16),
            pltpu.VMEM((COLS, GROUP, RHS), BF16),
            pltpu.VMEM((COLS, GROUP, RHS), BF16),
            pltpu.VMEM((OWN + 1, GROUP, RHS), F32),
            pltpu.VMEM((GROUP, RHS), F32),
            pltpu.VMEM((STEPS, 2, 3, SIDE, half, RHS), BF16),
            pltpu.VMEM((STEPS, 2, 3, SIDE, half, RHS), BF16),
            pltpu.VMEM((STEPS, 2, 3, half, RHS), F32),
            pltpu.VMEM((STEPS, 2, 3, half, RHS), F32),
            dma,
            dma,
            dma((STEPS, 2, 3)),
            dma((STEPS, 2, 3)),
            dma((STEPS, 2, 3)),
            dma((STEPS, 2, 3)),
            dma((STEPS - 1, 3)),
            dma((STEPS - 1, 3)),
            dma((STEPS - 1, SIDE)),
            dma((STEPS - 1, SIDE)),
        ],
        compiler_params=pltpu.CompilerParams(
            collective_id=0, has_side_effects=True, vmem_limit_bytes=VMEM_LIMIT
        ),
    )(perm, index, keep, last, slab, tiles, inverse, excitation)


def sorted_tables(tile_obs, tile_src, tile_lag):
    place = jnp.arange(OWN, dtype=jnp.int32)
    key = tile_obs * OWN + place
    rank = jnp.sum((key[None, :] < key[:, None]).astype(jnp.int32), axis=1)
    pick = (rank[None, :] == place[:, None]).astype(jnp.int32)
    perm = jnp.sum(pick * place[None, :], axis=1)
    obs = jnp.sum(pick * tile_obs[None, :], axis=1)
    src = jnp.sum(pick * tile_src[None, :], axis=1)
    lag = jnp.sum(pick * tile_lag[None, :], axis=1)
    before = jnp.concatenate([jnp.full((1,), -1, jnp.int32), obs[:-1]])
    keep = (obs == before).astype(F32)
    steps = jnp.arange(1, STEPS, dtype=jnp.int32)[:, None]
    index = jnp.where(lag[None, :] <= steps, (steps - lag[None, :]) * COLS + src[None, :], 3 * COLS)
    slabs = jnp.arange(ROWS, dtype=jnp.int32)
    upto = jnp.sum((tile_obs[None, :] <= slabs[:, None]).astype(jnp.int32), axis=1)
    count = jnp.sum((tile_obs[None, :] == slabs[:, None]).astype(jnp.int32), axis=1)
    last = jnp.where(count > 0, upto - 1, OWN)
    return perm, index.reshape(-1), keep, last


def swap_help(help_tiles, help_obs, help_src, help_lag, row, column):
    src = lax.dynamic_index_in_dim(help_src.reshape(ROWS, COLS, HELP), column, 1, keepdims=False)
    lag = lax.dynamic_index_in_dim(help_lag.reshape(ROWS, COLS, HELP), column, 1, keepdims=False)
    target = src // COLS
    order = jnp.arange(HELP, dtype=jnp.int32)
    earlier = (target[:, :, None] == target[:, None, :]) & (order[None, None, :] < order[None, :, None])
    slot = jnp.sum(earlier.astype(jnp.int32), axis=2)
    mine_target = lax.dynamic_index_in_dim(target, row, 0, keepdims=False)
    mine_slot = lax.dynamic_index_in_dim(slot, row, 0, keepdims=False)
    place = jnp.arange(POOL, dtype=jnp.int32)
    sends = (mine_target * CAP + mine_slot)[None, :] == place[:, None]
    pick = jnp.sum(jnp.where(sends, order[None, :], 0), axis=1)
    tiles_out = jnp.take(help_tiles, pick, axis=0).reshape(ROWS, CAP, GROUP, GROUP)
    pool = lax.all_to_all(tiles_out, "src", split_axis=0, concat_axis=0, tiled=True)
    every_obs = lax.all_gather(help_obs, "src", axis=0, tiled=False)
    slots = jnp.arange(CAP, dtype=jnp.int32)
    got = (target[:, None, :] == row) & (slot[:, None, :] == slots[None, :, None])
    ok = jnp.any(got, axis=2).astype(jnp.int32).reshape(-1)

    def gathered(values):
        return jnp.sum(jnp.where(got, values[:, None, :], 0), axis=2).reshape(-1)

    aid_lag = jnp.where(ok != 0, gathered(lag), LAGS)
    meta = (ok, gathered(every_obs), gathered(src % COLS), aid_lag)
    return pool.reshape(POOL, GROUP, GROUP), meta


def on_device(
    history, tiles, tile_obs, tile_src, tile_lag,
    help_tiles, help_obs, help_src, help_lag, self_inverse, excitation,
):
    row = lax.axis_index("src")
    column = lax.axis_index("obs")
    pool, aid_meta = swap_help(help_tiles, help_obs, help_src, help_lag, row, column)
    slab = history_fields((tile_obs, tile_src, tile_lag), aid_meta, history, tiles, pool)
    perm, index, keep, last = sorted_tables(tile_obs, tile_src, tile_lag)
    return march(perm, index, keep, last, slab, tiles, self_inverse, excitation)


def solution(mesh):
    placed = (
        P(None, "src", None, None),
        P(("src", "obs"), None, None),
        P(("src", "obs")),
        P(("src", "obs")),
        P(("src", "obs")),
        P(("src", "obs"), None, None),
        P(("src", "obs")),
        P(),
        P(),
        P(("src", "obs"), None, None),
        P(None, ("src", "obs"), None, None),
    )
    return jax.shard_map(
        on_device,
        mesh=mesh,
        in_specs=placed,
        out_specs=P(None, ("src", "obs"), None, None),
        check_vma=False,
    )
```

time: 751 us -> 306 us (0.41); the launches traced: 742 us -> 306 us
  waiting for transfers between devices: 357 us -> 0.01 us
  Pallas kernels: 0 us -> 150 us
  matrix products: 135 us -> 0 us
  local copies, waits for them, and re-layouts: 146 us -> 11.8 us
  blocking collectives: 50.9 us -> 124 us
  starting transfers between devices: 22 us -> 7.76 us
  between operations: 13.7 us -> 0.93 us
    unnamed x8 -> x0, waiting for transfers between devices: 299 us -> none
    pallas_call x0 -> x2, Pallas kernels: none -> 150 us  [the longest x1 118 us: march(): pl.pallas_call(march_kernel, out_shape=jax.ShapeDtypeStruct((STEPS, 1, GR...]
    dot_general x20 -> x0, matrix products: 135 us -> none  [the longest x4 50.6 us: on_device(): jnp.einsum('tab,tbr->tar', tiles, own_slices, preferred_element_type=jnp....]
    unnamed x0 -> x1, blocking collectives: none -> 124 us
    all_to_all x4 -> x1, waiting for transfers between devices: 57.6 us -> 0.01 us  [swap_help(): lax.all_to_all(tiles_out, 'src', split_axis=0, concat_axis=0, tiled=True)]
    gather x12 -> x1, local copies, waits for them, and re-layouts: 61.7 us -> 5.42 us  [swap_help(): jnp.take(help_tiles, pick, axis=0).reshape(ROWS, CAP, GROUP, GROUP)]
    all_gather x3 -> x0, blocking collectives: 50.9 us -> none  [on_device(): row_slices = lax.all_gather(solved, 'obs', axis=0, tiled=True)]
    dot_general x8 -> x0, local copies, waits for them, and re-layouts: 50.9 us -> none  [the longest x4 36.6 us: on_device(): jnp.einsum('tab,tbr->tar', tiles, own_slices, preferred_element_type=jnp....]
  transfers between devices with their start and end apart: 8 -> 1, of which waited for: 6 -> 0; matrix products, arithmetic and copies ran while one was open for 27% -> 2% of each run, Pallas kernels for 0% -> 0%
where the time goes in v1:
time: 306 us
  Pallas kernels  150 us (49%)
  blocking collectives  124 us (41%)
  local copies, waits for them, and re-layouts  11.8 us (4%)
  other arithmetic  11.4 us (4%)
  starting transfers between devices  7.76 us (3%)
    unnamed x1, blocking collectives  124 us
    pallas_call x1, Pallas kernels, march(): pl.pallas_call(march_kernel, out_shape=jax.ShapeDtypeStruct((STEPS, 1, GR...  118 us
    pallas_call x1, Pallas kernels, history_fields(): pl.pallas_call(history_kernel, out_shape=jax.ShapeDtypeStruct((ROWS, GROU...  32.2 us
    all_to_all x1, starting transfers between devices, swap_help(): lax.all_to_all(tiles_out, 'src', split_axis=0, concat_axis=0, tiled=True)  7.76 us
    select_n x2, other arithmetic, swap_help(): jnp.take(help_tiles, pick, axis=0).reshape(ROWS, CAP, GROUP, GROUP)  7.46 us
  transfers between devices with their start and end apart: 1, of which 0 were waited for; matrix products, arithmetic and copies ran while one was open for 2% of the time, Pallas kernels for 0%

profile of v1, /device:TPU:1, one launch (start us, length us, event | category | flops | bytes accessed | tf_op | source)
XLA Modules:
  0.0 306.0 jit_solution(1516870649342331550)
XLA Ops:
  0.0 0.9 reshape.115
  1.1 0.4 convert_reduce_fusion
  1.5 0.1 select_reduce_fusion.7
  1.8 0.2 copy-done
  1.9 5.4 %gather_fusion = bf16[64,256,256]{2,1,0:T(8,128)(2,1)} fusion(bf16[24,256,256]{2,1,0:T(8,128)(2,1)S(1)} %copy-done, s32[1024]{0:T(1024)S(1)} %pad_clamp_fusion), kind=kCustom, calls=%fused_computation | custom fusion | bytes 16777472 | tf_op jit(solution)/shard_map/jit(_take)/gather | solution.py:344
  7.3 7.5 %broadcast_select_fusion = bf16[16,4,256,256]{3,2,1,0:T(8,128)(2,1)} fusion(bf16[16,4,256,256]{3,2,1,0:T(8,128)(2,1)} %bitcast.17, pred[16,4]{1,0:T(8,128)(4,1)S(1)} %compare_and_fusion), kind=kLoop, calls=%fused_computation.1 | loop fusion | flops 4194304 | bytes 16777280 | tf_op jit(solution)/shard_map/jit(_take)/select_n | solution.py:344
  14.8 7.8 %all-to-all-start = ((bf16[16,4,256,256]{3,2,1,0:T(8,128)(2,1)}), bf16[16,4,256,256]{3,2,1,0:T(8,128)(2,1)}, u32[]{:S(2)}, u32[]{:S(2)}) async-start(bf16[16,4,256,256]{3,2,1,0:T(8,128)(2,1)} %broadcast_select_fusion), calls=%async_computation | async-start | bytes 16777216 | tf_op jit(solution)/shard_map/all_to_all | solution.py:345
  22.6 0.2 convert_reduce_fusion.1
  22.8 0.6 select_reduce_fusion.3
  23.5 0.6 select_n.84.index
  24.2 0.7 dynamic-slice
  25.5 0.2 dynamic-update-slice
  25.8 123.9 %all-reduce = s32[384]{0:T(512)S(1)} all-reduce(s32[384]{0:T(512)S(1)} %dynamic-update-slice), channel_id=2, replica_groups=mesh['src'=16,'obs'=8] {'src'}, use_global_device_ids=true, to_apply=%add | all-reduce | flops 384 | bytes 3072
  149.6 0.1 reshape.130
  149.7 0.1 fusion.1
  149.9 0.1 copy.12
  150.0 0.1 reshape.121.aid_ok
  150.1 0.1 reshape.118
  150.2 0.3 select_reduce_fusion
  150.5 0.1 copy.15
  150.6 0.1 reshape.119
  150.7 0.1 copy.14
  150.8 0.6 reshape.117.aid_src
  151.4 0.1 copy.13
  151.5 0.6 reshape.116.aid_obs
  152.1 0.1 convert_reduce_fusion.2
  152.2 0.7 compare_convert_fusion.keep
  152.9 0.5 compare_select_fusion.6.last
  153.4 0.6 compare_select_fusion.5.aid_lag
  154.0 32.2 %shard_map.109.slab_hbm = f32[16,256,512]{2,1,0:T(8,128)} custom-call(s32[64]{0:T(128)} %own_obs.1, s32[64]{0:T(128)} %own_src.1, s32[64]{0:T(128)} %own_lag.1, s32[64]{0:T(128)} %copy-done.2, s32[64]{0:T(128)} %reshape.116.aid_obs, s32[64]{0:T(128)} %reshape.117.aid_src, s32[64]{0:T(128)} %compare_select_fusion.5.aid_lag, bf16[8,8,256,128]{3,2,1,0:T(8,128)(2,1)} %history.1, ...), custom_call_target="tpu_custom_call" | custom-call | tf_op jit(solution)/shard_map/pallas_call | solution.py:86
  186.3 118.0 %shard_map.110 = bf16[4,1,256,128]{3,2,1,0:T(8,128)(2,1)} custom-call(s32[64]{0:T(128)} %get-tuple-element.13.perm, s32[192]{0:T(256)} %select_n.84.index, f32[64]{0:T(128)} %compare_convert_fusion.keep, s32[16]{0:T(128)} %compare_select_fusion.6.last, f32[16,256,512]{2,1,0:T(8,128)} %shard_map.109.slab_hbm, bf16[64,256,256]{2,1,0:T(8,128)(2,1)} %tiles_hbm.1, ...), custom_call_target="tpu_custom_call" | custom-call | tf_op jit(solution)/shard_map/pallas_call | solution.py:277
  304.3 1.7 copy.21
  (32 shorter events, 0.4 us)
Async XLA Ops:
  0.0 1.9 copy-start
  14.8 7.8 %copy-start.3 = (s32[64]{0:T(128)S(1)}, s32[64]{0:T(128)}, u32[]{:S(2)}) copy-start(s32[64]{0:T(128)} %own_obs.1) | copy-start | bytes 772
  14.8 8.0 %copy-start.4 = (s32[64]{0:T(128)S(1)}, s32[64]{0:T(128)}, u32[]{:S(2)}) copy-start(s32[64]{0:T(128)} %own_src.1) | copy-start | bytes 772
  14.8 8.0 %copy-start.5 = (s32[64]{0:T(128)S(1)}, s32[64]{0:T(128)}, u32[]{:S(2)}) copy-start(s32[64]{0:T(128)} %own_lag.1) | copy-start | bytes 772
  14.8 9.4 %copy-start.7 = (u32[128]{0:T(128)S(1)}, u32[128]{0:T(128)}, u32[]{:S(2)}) copy-start(u32[128]{0:T(128)} %constant.97) | copy-start | bytes 1540
  14.8 10.7 %copy-start.6 = (s32[24]{0:T(128)S(1)}, s32[24]{0:T(128)}, u32[]{:S(2)}) copy-start(s32[24]{0:T(128)} %param.17) | copy-start | bytes 292
  14.8 135.3 %copy-start.1 = (s32[3072]{0:T(1024)S(1)}, s32[3072]{0:T(1024)}, u32[]{:S(2)}) copy-start(s32[3072]{0:T(1024)} %param.19) | copy-start | bytes 36868
  14.8 139.2 %all-to-all-start = ((bf16[16,4,256,256]{3,2,1,0:T(8,128)(2,1)}), bf16[16,4,256,256]{3,2,1,0:T(8,128)(2,1)}, u32[]{:S(2)}, u32[]{:S(2)}) async-start(bf16[16,4,256,256]{3,2,1,0:T(8,128)(2,1)} %broadcast_select_fusion), calls=%async_computation | async-start | bytes 16777216 | tf_op jit(solution)/shard_map/all_to_all | solution.py:345
  150.1 3.9 %copy-start.2 = (s32[64]{0:T(128)}, s32[64]{0:T(128)S(1)}, u32[]{:S(2)}) copy-start(s32[64]{0:T(128)S(1)} %reshape.121.aid_ok) | copy-start | bytes 772

commit v2 on v1

--- a/solution.py
+++ b/solution.py
@@ -18,14 +18,215 @@
 HELP = 24
 CAP = 4
 POOL = ROWS * CAP
+ROUNDS = 22
+CHOICES = (19, 20, 22)
+SLOTS = HELP + 8 + 4 * ROUNDS
 MESH = pl.DeviceIdType.MESH
 F32 = jnp.float32
 BF16 = jnp.bfloat16
 VMEM_LIMIT = 60 * 2**20
 
 
+def plan_kernel(src, lag, moves, final, rounds, state):
+    lane = lax.broadcasted_iota(jnp.int32, (HELP, ROWS * COLS), 1)
+    tile = lax.broadcasted_iota(jnp.int32, (HELP, ROWS * COLS), 0)
+    row = lane // COLS
+    target = src[...] // COLS
+    left_x = (target % SIDE - row % SIDE) & 3
+    left_y = (target // SIDE - row // SIDE) & 3
+    state[pl.ds(0, HELP)] = (
+        left_x | (left_y << 2) | (((row << 5) | tile) << 4)
+        | ((src[...] % COLS) << 13) | ((lag[...] - 3) << 16)
+    )
+    state[pl.ds(HELP, SLOTS - HELP)] = jnp.zeros((SLOTS - HELP, ROWS * COLS), jnp.int32)
+    slot = lax.broadcasted_iota(jnp.int32, (SLOTS, ROWS * COLS), 0)
+    one = lax.broadcasted_iota(jnp.int32, (1, ROWS * COLS), 1)
+    x_here = (one // COLS) % SIDE
+
+    def link(number, now):
+        along, up = number < 2, number % 2 == 0
+        left = now & 3 if along else (now >> 2) & 3
+        rest = (now >> 2) & 3 if along else now & 3
+        may = (left == (1 if up else 3)) | (left == 2)
+        hops = jnp.where(left == 3, 1, left) + jnp.where(rest == 3, 1, rest)
+        rank = hops * 4 + jnp.where(rest == 0, 2, 0) + jnp.where(left == 2, 0, 1)
+        key = jnp.where(may, (rank << 26) | (slot << 19) | now, 0)
+        best = jnp.max(key, axis=0, keepdims=True)
+        now = jnp.where(may & (key == best), 0, now)
+        record = best & ((1 << 19) - 1)
+        step = -1 if up else 1
+        if along:
+            record = (record & ~3) | ((record + step) & 3)
+        else:
+            record = (record & ~12) | ((record + 4 * step) & 12)
+        record = jnp.where(best > 0, record, 0)
+        if along:
+            near = pltpu.roll(record, COLS if up else ROWS * COLS - COLS, 1)
+            wrap = pltpu.roll(record, ROWS * COLS - 3 * COLS if up else 3 * COLS, 1)
+            record = jnp.where(x_here == (0 if up else SIDE - 1), wrap, near)
+        else:
+            shift = SIDE * COLS
+            record = pltpu.roll(record, shift if up else ROWS * COLS - shift, 1)
+        return now, record, jnp.where(best > 0, (best >> 19) & 127, 0), best > 0
+
+    def one_round(t, order, carry):
+        used, older, old = carry
+        for i in range(4):
+            state[pl.ds(HELP + 4 * t + i, 1)] = older[i]
+        now = state[...]
+        fresh = [None] * 4
+        for number in order:
+            now, fresh[number], pick, moved = link(number, now)
+            moves[pl.ds(4 * t + number, 1)] = pick
+            used = jnp.where(moved, t + 1, used)
+        state[...] = now
+        return used, old, tuple(fresh)
+
+    def two_rounds(i, carry):
+        carry = one_round(2 * i, (0, 1, 2, 3), carry)
+        return one_round(2 * i + 1, (2, 3, 0, 1), carry)
+
+    empty = jnp.zeros((1, ROWS * COLS), jnp.int32)
+    none = (empty,) * 4
+    used, older, old = lax.fori_loop(0, ROUNDS // 2, two_rounds, (empty, none, none))
+    for i in range(4):
+        state[pl.ds(HELP + 4 * ROUNDS + i, 1)] = older[i]
+        state[pl.ds(HELP + 4 * ROUNDS + 4 + i, 1)] = old[i]
+    now = state[...]
+    final[...] = now[HELP + 8 :]
+    rounds[0] = jnp.max(used) + ROUNDS * jnp.max(jnp.where((now & 15) != 0, 1, 0))
+
+
+def plan_routes(src, lag):
+    vmem = pl.BlockSpec(memory_space=pltpu.VMEM)
+    shape = jax.ShapeDtypeStruct((4 * ROUNDS, ROWS * COLS), jnp.int32)
+    return pl.pallas_call(
+        plan_kernel,
+        out_shape=(shape, shape, jax.ShapeDtypeStruct((1,), jnp.int32)),
+        in_specs=[vmem] * 2,
+        out_specs=(vmem, vmem, pl.BlockSpec(memory_space=pltpu.SMEM)),
+        scratch_shapes=[pltpu.VMEM((SLOTS, ROWS * COLS), jnp.int32)],
+    )(src, lag)
+
+
+def route_kernel(
+    rounds, moves, help_tiles, help_obs, out, every_obs,
+    pool, landed, stage, obs_in, sem_in, sem_out, s_tx, s_rx, s_otx, s_orx,
+):
+    row = lax.axis_index("src")
+    col = lax.axis_index("obs")
+    y, x = row // SIDE, lax.rem(row, SIDE)
+
+    def at(dy, dx):
+        return (lax.rem(y + dy, SIDE) * SIDE + lax.rem(x + dx, SIDE), col)
+
+    others = [(dy, dx) for dy in range(SIDE) for dx in range(SIDE) if (dy, dx) != (0, 0)]
+    links = [at(0, 1), at(0, SIDE - 1), at(1, 0), at(SIDE - 1, 0)]
+    fetch = pltpu.make_async_copy(help_tiles, pool.at[pl.ds(0, HELP)], sem_in)
+    fetch.start()
+    barrier = pltpu.get_barrier_semaphore()
+    for dy, dx in others:
+        pl.semaphore_signal(barrier, inc=1, device_id=at(dy, dx), device_id_type=MESH)
+    pool[pl.ds(HELP, 8)] = jnp.zeros((8, GROUP, GROUP), BF16)
+    obs_in[row] = help_obs[...]
+    fetch.wait()
+    pl.semaphore_wait(barrier, len(others))
+    notes = []
+    for i, (dy, dx) in enumerate(others):
+        note = pltpu.make_async_remote_copy(
+            src_ref=help_obs,
+            dst_ref=obs_in.at[row],
+            send_sem=s_otx.at[i],
+            recv_sem=s_orx.at[i],
+            device_id=at(dy, dx),
+            device_id_type=MESH,
+        )
+        note.start()
+        notes.append(note)
+
+    def hop(t, number):
+        place = lax.rem(t, 2) * 4 + number
+        return pltpu.make_async_remote_copy(
+            src_ref=stage.at[place],
+            dst_ref=landed.at[4 * t + number],
+            send_sem=s_tx.at[place],
+            recv_sem=s_rx.at[4 * t + number],
+            device_id=links[number],
+            device_id_type=MESH,
+        )
+
+    def keep(t, number):
+        return pltpu.make_async_copy(
+            landed.at[4 * t + number], out.at[4 * t + number], sem_out.at[4 * t + number]
+        )
+
+    def send(t):
+        for number in range(4):
+            stage[lax.rem(t, 2) * 4 + number] = pool[moves[4 * t + number]]
+            hop(t, number).start()
+
+    def take(t):
+        for number in range(4):
+            hop(t, number).wait_recv()
+            keep(t, number).start()
+
+    send(0)
+    send(1)
+
+    @pl.loop(2, rounds)
+    def _(t):
+        take(t - 2)
+        for number in range(4):
+            pool[HELP + 8 + 4 * (t - 2) + number] = landed[4 * (t - 2) + number]
+            hop(t - 2, number).wait_send()
+        send(t)
+
+    for t in (rounds - 2, rounds - 1):
+        take(t)
+        for number in range(4):
+            hop(t, number).wait_send()
+    for note in notes:
+        note.wait()
+    every_obs[...] = obs_in[...]
+
+    @pl.loop(0, rounds)
+    def _(t):
+        for number in range(4):
+            keep(t, number).wait()
+
+
+def route(rounds, collective, moves, help_tiles, help_obs):
+    vmem = pl.BlockSpec(memory_space=pltpu.VMEM)
+    hbm = pl.BlockSpec(memory_space=pl.ANY)
+    dma = pltpu.SemaphoreType.DMA
+    return pl.pallas_call(
+        functools.partial(route_kernel, rounds),
+        out_shape=(
+            jax.ShapeDtypeStruct((4 * ROUNDS, GROUP, GROUP), BF16),
+            jax.ShapeDtypeStruct((ROWS, 8, 128), jnp.int32),
+        ),
+        in_specs=[pl.BlockSpec(memory_space=pltpu.SMEM), hbm, vmem],
+        out_specs=(hbm, vmem),
+        scratch_shapes=[
+            pltpu.VMEM((HELP + 8 + 4 * rounds, GROUP, GROUP), BF16),
+            pltpu.VMEM((4 * rounds, GROUP, GROUP), BF16),
+            pltpu.VMEM((8, GROUP, GROUP), BF16),
+            pltpu.VMEM((ROWS, 8, 128), jnp.int32),
+            dma,
+            dma((4 * rounds,)),
+            dma((8,)),
+            dma((4 * rounds,)),
+            dma((ROWS - 1,)),
+            dma((ROWS - 1,)),
+        ],
+        compiler_params=pltpu.CompilerParams(
+            collective_id=collective, has_side_effects=True, vmem_limit_bytes=VMEM_LIMIT
+        ),
+    )(moves, help_tiles, help_obs)
+
+
 def history_kernel(
-    own_obs, own_src, own_lag, aid_ok, aid_obs, aid_src, aid_lag,
+    own_obs, own_src, own_lag, aid, aid_obs,
     history, tiles, pool, out, past, own_buf, aid_buf, acc, sem_past, sem_own, sem_aid, sem_out,
 ):
     chunk = 8
@@ -41,14 +242,21 @@
         )
         for i in range(OWN // chunk)
     ]
-    aid_copies = [
-        pltpu.make_async_copy(
-            pool.at[pl.ds(i * chunk, chunk)], aid_buf.at[pl.ds(i * chunk, chunk)], sem_aid.at[i]
-        )
-        for i in range(POOL // chunk)
-    ]
-    for copy in past_copies + own_copies + aid_copies:
+    for copy in past_copies + own_copies:
         copy.start()
+
+    def arrived(t):
+        return (aid[t] != 0) & ((aid[t] & 15) == 0)
+
+    def aid_copy(t):
+        return pltpu.make_async_copy(pool.at[t], aid_buf.at[t], sem_aid.at[t])
+
+    @pl.loop(0, 4 * ROUNDS)
+    def _(t):
+        @pl.when(arrived(t))
+        def _():
+            aid_copy(t).start()
+
     past[:, :, pl.ds(LAGS * RHS, 3 * RHS)] = jnp.zeros((COLS, GROUP, 3 * RHS), BF16)
     acc[...] = jnp.zeros(acc.shape, F32)
     for copy in past_copies:
@@ -66,40 +274,40 @@
         def _(t):
             add(own_buf[t], own_obs[t], own_src[t], own_lag[t])
 
-    for i in range(POOL // chunk):
-        aid_copies[i].wait()
-
-        @pl.loop(i * chunk, (i + 1) * chunk)
-        def _(t):
-            @pl.when(aid_ok[t] != 0)
-            def _():
-                add(aid_buf[t], aid_obs[t], aid_src[t], aid_lag[t])
+    @pl.loop(0, 4 * ROUNDS)
+    def _(t):
+        @pl.when(arrived(t))
+        def _():
+            note = aid[t]
+            aid_copy(t).wait()
+            obs = aid_obs[(note >> 9) & 15, (note >> 4) & 31]
+            add(aid_buf[t], obs, (note >> 13) & 7, ((note >> 16) & 7) + 3)
 
     copy = pltpu.make_async_copy(acc, out, sem_out)
     copy.start()
     copy.wait()
 
 
-def history_fields(own_meta, aid_meta, history, tiles, pool):
+def history_fields(own_meta, aid, aid_obs, history, tiles, pool):
     smem = pl.BlockSpec(memory_space=pltpu.SMEM)
     hbm = pl.BlockSpec(memory_space=pl.ANY)
     return pl.pallas_call(
         history_kernel,
         out_shape=jax.ShapeDtypeStruct((ROWS, GROUP, STEPS * RHS), F32),
-        in_specs=[smem] * 7 + [hbm] * 3,
+        in_specs=[smem] * 5 + [hbm] * 3,
         out_specs=hbm,
         scratch_shapes=[
             pltpu.VMEM((COLS, GROUP, (LAGS + 3) * RHS), BF16),
             pltpu.VMEM((OWN, GROUP, GROUP), BF16),
-            pltpu.VMEM((POOL, GROUP, GROUP), BF16),
+            pltpu.VMEM((4 * ROUNDS, GROUP, GROUP), BF16),
             pltpu.VMEM((ROWS, GROUP, STEPS * RHS), F32),
             pltpu.SemaphoreType.DMA((LAGS,)),
             pltpu.SemaphoreType.DMA((OWN // 8,)),
-            pltpu.SemaphoreType.DMA((POOL // 8,)),
+            pltpu.SemaphoreType.DMA((4 * ROUNDS,)),
             pltpu.SemaphoreType.DMA,
         ],
         compiler_params=pltpu.CompilerParams(vmem_limit_bytes=VMEM_LIMIT),
-    )(*own_meta, *aid_meta, history, tiles, pool)
+    )(*own_meta, aid, aid_obs, history, tiles, pool)
 
 
 def march_kernel(
@@ -346,14 +554,12 @@
     every_obs = lax.all_gather(help_obs, "src", axis=0, tiled=False)
     slots = jnp.arange(CAP, dtype=jnp.int32)
     got = (target[:, None, :] == row) & (slot[:, None, :] == slots[None, :, None])
-    ok = jnp.any(got, axis=2).astype(jnp.int32).reshape(-1)
-
-    def gathered(values):
-        return jnp.sum(jnp.where(got, values[:, None, :], 0), axis=2).reshape(-1)
-
-    aid_lag = jnp.where(ok != 0, gathered(lag), LAGS)
-    meta = (ok, gathered(every_obs), gathered(src % COLS), aid_lag)
-    return pool.reshape(POOL, GROUP, GROUP), meta
+    rows = jnp.arange(ROWS, dtype=jnp.int32)
+    note = (((rows[:, None] << 5) | order[None, :]) << 4) | ((src % COLS) << 13) | ((lag - 3) << 16)
+    aid = jnp.sum(jnp.where(got, note[:, None, :], 0), axis=2).reshape(-1)
+    spare = 4 * ROUNDS - POOL
+    pool = jnp.pad(pool.reshape(POOL, GROUP, GROUP), ((0, spare), (0, 0), (0, 0)))
+    return pool, jnp.pad(every_obs, ((0, 0), (0, 128 - HELP))), jnp.pad(aid, (0, spare))
 
 
 def on_device(
@@ -362,8 +568,28 @@
 ):
     row = lax.axis_index("src")
     column = lax.axis_index("obs")
-    pool, aid_meta = swap_help(help_tiles, help_obs, help_src, help_lag, row, column)
-    slab = history_fields((tile_obs, tile_src, tile_lag), aid_meta, history, tiles, pool)
+    moves, final, rounds = plan_routes(
+        help_src.reshape(ROWS * COLS, HELP).T, help_lag.reshape(ROWS * COLS, HELP).T
+    )
+    lane = row * COLS + column
+    own_moves = lax.dynamic_index_in_dim(moves, lane, 1, keepdims=False)
+    own_final = lax.dynamic_index_in_dim(final, lane, 1, keepdims=False)
+
+    def routed(count, collective):
+        def run():
+            own_obs = jnp.zeros((8, 128), jnp.int32).at[0, :HELP].set(help_obs)
+            pool, every_obs = route(count, collective, own_moves, help_tiles, own_obs)
+            return pool, every_obs[:, 0, :], own_final
+
+        return run
+
+    def general():
+        return swap_help(help_tiles, help_obs, help_src, help_lag, row, column)
+
+    branches = [routed(count, 1 + i) for i, count in enumerate(CHOICES)] + [general]
+    choice = sum((rounds[0] > count).astype(jnp.int32) for count in CHOICES)
+    pool, every_obs, aid = lax.switch(choice, branches)
+    slab = history_fields((tile_obs, tile_src, tile_lag), aid, every_obs, history, tiles, pool)
     perm, index, keep, last = sorted_tables(tile_obs, tile_src, tile_lag)
     return march(perm, index, keep, last, slab, tiles, self_inverse, excitation)
 

time: 306 us -> 237 us (0.77)
  blocking collectives: 124 us -> 0 us
  Pallas kernels: 150 us -> 224 us
  other arithmetic: 11.4 us -> 2.15 us
  starting transfers between devices: 7.76 us -> 0 us
  local copies, waits for them, and re-layouts: 11.8 us -> 8.05 us
    unnamed x1 -> x0, blocking collectives: 124 us -> none
    pallas_call x0 -> x2, Pallas kernels: none -> 73.6 us  [the longest x1 65.7 us: route(): pl.pallas_call(functools.partial(route_kernel, rounds), out_shape=(jax.Sh...]
    select_n x5 -> x0, other arithmetic: 8.1 us -> none  [the longest x2 7.46 us: swap_help(): jnp.take(help_tiles, pick, axis=0).reshape(ROWS, CAP, GROUP, GROUP)]
    all_to_all x1 -> x0, starting transfers between devices: 7.76 us -> none  [swap_help(): lax.all_to_all(tiles_out, 'src', split_axis=0, concat_axis=0, tiled=True)]
    gather x1 -> x0, local copies, waits for them, and re-layouts: 5.42 us -> none  [swap_help(): jnp.take(help_tiles, pick, axis=0).reshape(ROWS, CAP, GROUP, GROUP)]
  transfers between devices with their start and end apart: 1 -> 0, of which waited for: 0 -> 0; matrix products, arithmetic and copies ran while one was open for 2% -> 0% of each run, Pallas kernels for 0% -> 0%
where the time goes in v2:
time: 237 us
  Pallas kernels  224 us (95%)
  local copies, waits for them, and re-layouts  8.05 us (3%)
    pallas_call x1, Pallas kernels, march(): pl.pallas_call(march_kernel, out_shape=jax.ShapeDtypeStruct((STEPS, 1, GR...  119 us
    pallas_call x1, Pallas kernels, route(): pl.pallas_call(functools.partial(route_kernel, rounds), out_shape=(jax.Sh...  65.7 us
    pallas_call x1, Pallas kernels, history_fields(): pl.pallas_call(history_kernel, out_shape=jax.ShapeDtypeStruct((ROWS, GROU...  31.8 us
    pallas_call x1, Pallas kernels, plan_routes(): pl.pallas_call(plan_kernel, out_shape=(shape, shape, jax.ShapeDtypeStruct...  7.96 us

profile of v2, /device:TPU:1, one launch (start us, length us, event | category | flops | bytes accessed | tf_op | source)
XLA Modules:
  0.0 236.5 jit_solution(8046100528317126901)
XLA Ops:
  0.0 0.8 reshape.246
  0.8 0.7 copy.46
  1.5 0.8 reshape.247
  2.3 0.7 copy.47
  2.9 8.0 %shard_map.109 = (s32[88,128]{1,0:T(8,128)S(1)}, s32[88,128]{1,0:T(8,128)S(1)}, s32[1]{0:T(128)}) custom-call(s32[24,128]{1,0:T(8,128)} %bitcast.45, s32[24,128]{1,0:T(8,128)} %bitcast.46), custom_call_target="tpu_custom_call" | custom-call | tf_op jit(solution)/shard_map/pallas_call | solution.py:103
  12.6 68.5 %conditional.1 = (bf16[88,256,256]{2,1,0:T(8,128)(2,1)}, s32[16,128]{1,0:T(8,128)S(1)}, s32[88]{0:T(128)S(1)}) conditional(s32[]{:T(128)} %bitcast.24, (s32[24]{0:T(128)}, s32[88,128]{1,0:T(8,128)S(1)}, bf16[24,256,256]{2,1,0:T(8,128)(2,1)}, s32[88,128]{1,0:T(8,128)S(1)}, s32[]{:T(128)}, /*index=5*/s32[]{:T(128)}, ...), branch_computations={%region_7.8_spmd, %region_8.9_spmd, %region_9.10_spmd, %region_10.... | conditional | flops 4265929 | bytes 78747800 | solution.py:591
  12.6 0.1 copy.50
  12.7 0.1 copy.51
  12.8 0.5 dynamic-slice_bitcast_fusion.2
  13.3 1.3 scatter.7.help_obs
  14.6 65.7 %branch_1_fun.1 = (bf16[88,256,256]{2,1,0:T(8,128)(2,1)}, s32[16,8,128]{2,1,0:T(8,128)}) custom-call(s32[88]{0:T(128)} %get-tuple-element.266.moves, bf16[24,256,256]{2,1,0:T(8,128)(2,1)} %get-tuple-element.84.help_tiles, s32[8,128]{1,0:T(8,128)} %scatter.7.help_obs), custom_call_target="tpu_custom_call" | custom-call | tf_op jit(solution)/shard_map/cond/branch_1_fun/pallas_call | solution.py:202
  80.3 0.8 slice.57
  81.1 0.0 copy-start.3
  81.1 0.0 copy-start.1
  81.1 0.0 copy-start.2
  81.1 31.8 %shard_map.110.slab_hbm = f32[16,256,512]{2,1,0:T(8,128)} custom-call(s32[64]{0:T(128)} %own_obs.1, s32[64]{0:T(128)} %own_src.1, s32[64]{0:T(128)} %own_lag.1, s32[88]{0:T(128)S(1)} %get-tuple-element.110.aid, s32[16,128]{1,0:T(8,128)S(1)} %get-tuple-element.111.aid_obs, bf16[8,8,256,128]{3,2,1,0:T(8,128)(2,1)} %history.1, bf16[64,256,256]{2,1,0:T(8,128)(2,1)} %tiles_hbm.1, ...), custom_call_target="tpu_custom_call" | custom-call | tf_op jit(solution)/shard_map/pallas_call | solution.py:294
  113.0 0.0 copy-done.3
  113.0 0.2 convert_reduce_fusion.1
  113.2 0.0 copy-done.1
  113.2 0.0 copy-done.2
  113.2 0.7 select_reduce_fusion.2
  113.9 0.6 compare_convert_fusion.keep
  114.5 0.1 add_select_fusion.3
  114.6 0.6 select_n.79.index
  115.2 0.1 convert_reduce_fusion.2
  115.3 0.5 compare_select_fusion.2.last
  115.8 119.0 %shard_map.111 = bf16[4,1,256,128]{3,2,1,0:T(8,128)(2,1)} custom-call(s32[64]{0:T(128)} %get-tuple-element.262.perm, s32[192]{0:T(256)} %select_n.79.index, f32[64]{0:T(128)} %compare_convert_fusion.keep, s32[16]{0:T(128)} %compare_select_fusion.2.last, f32[16,256,512]{2,1,0:T(8,128)} %shard_map.110.slab_hbm, bf16[64,256,256]{2,1,0:T(8,128)(2,1)} %tiles_hbm.1, ...), custom_call_target="tpu_custom_call" | custom-call | tf_op jit(solution)/shard_map/pallas_call | solution.py:485
  234.9 1.7 copy.70
  (2 shorter events, 0.0 us)
Async XLA Ops:
  81.1 31.8 %copy-start.3 = (s32[64]{0:T(128)S(1)}, s32[64]{0:T(128)}, u32[]{:S(2)}) copy-start(s32[64]{0:T(128)} %own_obs.1) | copy-start | bytes 772
  81.1 32.0 %copy-start.1 = (s32[64]{0:T(128)S(1)}, s32[64]{0:T(128)}, u32[]{:S(2)}) copy-start(s32[64]{0:T(128)} %own_src.1) | copy-start | bytes 772
  81.1 32.0 %copy-start.2 = (s32[64]{0:T(128)S(1)}, s32[64]{0:T(128)}, u32[]{:S(2)}) copy-start(s32[64]{0:T(128)} %own_lag.1) | copy-start | bytes 772
